TPU v7x, 32 devices: a whole 2x2x4 slice. The times are simulated.
32 devices in a mesh: tm: 8 (over z, y), space: 4 (over x, core).
Axes of the slice: x: 2, y: 2, z: 4, core: 2. Of those that a mesh axis runs over, the one named last changes fastest.
Arguments:
- snapshots: bfloat16 [4096, 3, 4096], P('tm', None, 'space'), may hold values from -6 to 6
- cell_weights: float32 [4096], P('space'), may hold values from 0.25 to 4
- triads: int32 [64, 3], replicated, may hold values from 0 to 127, as said below
- owner_slots: int32 [8, 16], replicated, may hold values from -1 to 63, as said below
Outputs:
- bispectra: float32 [128, 512], P(('tm', 'space'))
Inputs may be any that keep to these rules, and one draw needn't show every extreme that they name: `triads`: every row is (k, l, k + l); all three entries are below 128. `owner_slots`: every triad index stands in exactly one slot of the table; in each row the used slots come first and the others hold -1; some owner fills all 16 slots.
All inputs are finite; a program needn't handle non-finite values.
Results may differ from a plain program's by a relative error of at most 0.0076.
Values may be sent and summed in bfloat16 or wider, within the bound.
A program may use at most 64 MiB of HBM per device.

v0:
```python
import functools
import math

import jax
import jax.numpy as jnp
import ml_dtypes
import numpy as np
from jax import lax
from jax.experimental import pallas as pl
from jax.experimental.pallas import tpu as pltpu
from jax.sharding import PartitionSpec as P

NB = 16
NT = 256
K = 128
GROUP = 8
LANES = 128
MESH = pl.DeviceIdType.MESH


def spectral_table():
    sample = np.arange(NT)
    freq_bins = np.arange(K)
    angles = 2.0 * math.pi / NT * (freq_bins[:, None] * sample[None, :] % NT)
    window = 0.5 - 0.5 * np.cos(2.0 * math.pi / NT * sample)
    scale = math.sqrt(8.0 / (3.0 * NT))
    rows = np.stack(
        [scale * window * np.cos(angles), -scale * window * np.sin(angles)], axis=1
    )
    return rows.reshape(2 * K, NT).astype(np.float32).astype(ml_dtypes.bfloat16)


def choose(ns, sizes, triads, slots, place, freqs, filled, which):
    wide = 2 * K
    ntri = triads.shape[1]
    owners, per = slots.shape
    nslot = owners * per
    mine = per // ns
    slot_of = lax.broadcasted_iota(jnp.int32, (per, nslot), 0)
    lane = lax.broadcasted_iota(jnp.int32, (per, nslot), 1)
    repeat = jnp.where(lane % per == slot_of, 1.0, 0.0).astype(jnp.bfloat16)
    held = slots[...].astype(jnp.float32)
    wide_slots = jnp.dot(
        held.astype(jnp.bfloat16), repeat, preferred_element_type=jnp.float32
    )
    owner_row = lax.broadcasted_iota(jnp.int32, (owners, nslot), 0)
    lane_owner = lax.broadcasted_iota(jnp.int32, (owners, nslot), 1) // per
    slot_row = jnp.sum(
        jnp.where(owner_row == lane_owner, wide_slots, 0.0), axis=0, keepdims=True
    ).astype(jnp.int32)
    full = jnp.where(held >= 0.0, 1.0, 0.0).astype(jnp.bfloat16)
    slot_of = lax.broadcasted_iota(jnp.int32, (per, LANES), 0)
    lane = lax.broadcasted_iota(jnp.int32, (per, LANES), 1)
    for j in range(ns):
        spot = jnp.where(slot_of == j * mine + (lane // NB) % mine, 1.0, 0.0)
        filled[j] = jnp.dot(
            full, spot.astype(jnp.bfloat16), preferred_element_type=jnp.float32
        )
    bin_of = lax.broadcasted_iota(jnp.int32, (wide, ntri), 0) // 2
    hit = (triads[0:1] == bin_of) | (triads[1:2] == bin_of) | (triads[2:3] == bin_of)
    hit = jnp.where(hit, 1.0, 0.0).astype(jnp.bfloat16)
    ones = jnp.ones((16, ntri), jnp.bfloat16)
    hits = lax.dot_general(
        ones, hit, (((1,), (1,)), ((), ())), preferred_element_type=jnp.float32
    )
    used = jnp.where(hits > 0.5, 1.0, 0.0)
    row = lax.broadcasted_iota(jnp.int32, (wide, wide), 0)
    column = lax.broadcasted_iota(jnp.int32, (wide, wide), 1)
    before = jnp.where(row < column, 1.0, 0.0).astype(jnp.bfloat16)
    rank = jnp.dot(used.astype(jnp.bfloat16), before, preferred_element_type=jnp.float32)
    place[...] = jnp.where(used > 0.5, rank, -1.0)[0:1].astype(jnp.int32)
    triad_row = lax.broadcasted_iota(jnp.int32, (ntri, nslot), 0)
    of_slot = jnp.where(triad_row == slot_row, 1.0, 0.0).astype(jnp.bfloat16)
    bin_row = lax.broadcasted_iota(jnp.int32, (wide, nslot), 0)
    rank = rank.astype(jnp.bfloat16)
    for i in range(3):
        tri = jnp.broadcast_to(triads[i : i + 1].astype(jnp.float32), (16, ntri))
        freq = jnp.dot(
            tri.astype(jnp.bfloat16), of_slot, preferred_element_type=jnp.float32
        )
        same = bin_row == 2 * freq[0:1].astype(jnp.int32)
        same = jnp.where(same, 1.0, 0.0).astype(jnp.bfloat16)
        twice = jnp.dot(rank, same, preferred_element_type=jnp.float32)
        freqs[i : i + 1, :] = (twice[0:1] * 0.5).astype(jnp.int32)
    need = jnp.sum(used[0:1]) * 0.5
    branch = jnp.int32(0)
    for size in sizes[:-1]:
        branch = branch + (need > size + 0.5).astype(jnp.int32)
    which[0, 0] = branch


def kernel(
    n,
    ns,
    weight_scale,
    bins,
    snap,
    table,
    place,
    weights,
    freqs,
    filled,
    out,
    whole,
    picked,
    local,
    stage,
    recv,
    rows,
    spec,
    narrow,
    acc,
    part,
    summed,
    last,
    send_sem,
    recv_sem,
    own_sem,
    table_sem,
    send1,
    recv1,
    send2,
    recv2,
):
    comps, times = snap.shape[0], snap.shape[1]
    me = lax.axis_index("tm")
    col = lax.axis_index("space")
    first = times % NT == 0
    blocks = times // NT

    def partner(place, m, size):
        other, bit = 0, 1
        while bit < size:
            other = other + lax.rem(place // bit + m // bit, 2) * bit
            bit *= 2
        return other

    def turn(i):
        i = lax.rem(i + lax.rem(col, 2) * (n // 2), n - 1)
        return (i + 1) // 2 + (1 - lax.rem(i, 2)) * (n // 2)

    def load(c):
        return pltpu.make_async_copy(snap.at[c], local.at[c], own_sem.at[c])

    fetch = pltpu.make_async_copy(table, whole, table_sem)
    fetch.start()
    if first:
        for c in range(comps):
            load(c).start()

    barrier = pltpu.get_barrier_semaphore()

    def greet_tm(off, carry):
        pl.semaphore_signal(
            barrier, inc=1, device_id=(partner(me, off, n), col), device_id_type=MESH
        )
        return carry

    lax.fori_loop(1, n, greet_tm, 0)
    for off in range(1, ns):
        pl.semaphore_signal(
            barrier, inc=1, device_id=(me, partner(col, off, ns)), device_id_type=MESH
        )
    fetch.wait()
    if first:
        row = lax.broadcasted_iota(jnp.int32, picked.shape, 0)
        pick = jnp.where(row == place[...], 1.0, 0.0).astype(jnp.bfloat16)
        picked[...] = jnp.dot(
            pick, whole[...], preferred_element_type=jnp.float32
        ).astype(jnp.bfloat16)
    pl.semaphore_wait(barrier, n - 1 + ns - 1)

    def exchange(c, off):
        peer = partner(me, off, n)
        if first:
            return pltpu.make_async_remote_copy(
                src_ref=stage.at[c, off],
                dst_ref=recv.at[c, off],
                send_sem=send_sem.at[c, off],
                recv_sem=recv_sem.at[c, off],
                device_id=(peer, col),
                device_id_type=MESH,
            )
        return pltpu.make_async_remote_copy(
            src_ref=snap.at[c, :, pl.ds(pl.multiple_of(peer * LANES, LANES), LANES)],
            dst_ref=recv.at[c, pl.ds(pl.multiple_of(me * times, 16), times), :],
            send_sem=send_sem.at[c, off],
            recv_sem=recv_sem.at[c, off],
            device_id=(peer, col),
            device_id_type=MESH,
        )

    def own(c):
        return pltpu.make_async_copy(
            snap.at[c, :, pl.ds(pl.multiple_of(me * LANES, LANES), LANES)],
            recv.at[c, pl.ds(pl.multiple_of(me * times, 16), times), :],
            own_sem.at[c],
        )

    def spectra(c, off):
        peer = partner(me, off, n)
        parts = []
        for i in range(blocks):
            x = local[
                c, i * NT : (i + 1) * NT, pl.ds(pl.multiple_of(peer * LANES, LANES), LANES)
            ]
            y = jnp.dot(picked[...], x, preferred_element_type=jnp.float32)
            parts.append(y[: 2 * bins])
        stage[c, off] = jnp.concatenate(parts, axis=0).astype(jnp.bfloat16)

    for c in range(comps):
        if first:
            load(c).wait()

        def begin(i, carry, c=c):
            off = turn(i)
            if first:
                spectra(c, off)
            exchange(c, off).start()
            return carry

        lax.fori_loop(0, n - 1, begin, 0)
        if not first:
            own(c).start()

    w_row = weights[pl.ds(me, 1), :] * weight_scale
    lane = lax.broadcasted_iota(jnp.int32, (2 * NB, 2 * LANES), 1)
    lane_group = lax.rem(lane, LANES) // NB
    low = lax.broadcasted_iota(jnp.int32, (NB, LANES), 1) < LANES // 2
    groups = freqs.shape[1] // GROUP
    per_owner = groups // n

    def dft(c, b):
        x = recv[c, pl.ds(pl.multiple_of(b * NT, NT), NT), :]
        y = jnp.dot(whole[...], x, preferred_element_type=jnp.float32)
        rows[pl.ds(b, 2 * K, stride=NB), :] = y

    def regroup(k, carry):
        both = rows[pl.ds(pl.multiple_of(k * 2 * NB, 2 * NB), 2 * NB), :].astype(jnp.bfloat16)
        narrow[k] = both
        spec[k] = both.astype(jnp.float32)
        return carry

    def spread(c, off, source):
        src = partner(me, off, n)
        both = source[c, off].astype(jnp.float32)
        for i in range(blocks):
            part_rows = both[i * 2 * bins : (i + 1) * 2 * bins]
            rows[pl.ds(src * blocks + i, 2 * bins, stride=NB), :] = part_rows

    def gram_group(c, owner, half):
        g = owner * per_owner + half
        prods, c_re, c_im = [], [], []
        for s in range(GROUP):
            place = g * GROUP + s
            a = spec[freqs[0, place]]
            b2 = spec[freqs[1, place]]
            c2 = narrow[freqs[2, place]]
            re = (a[:NB] * b2[:NB] - a[NB:] * b2[NB:]) * w_row
            im = (a[:NB] * b2[NB:] + a[NB:] * b2[:NB]) * w_row
            prods += [re.astype(jnp.bfloat16), im.astype(jnp.bfloat16)]
            c_re.append(c2[:NB])
            c_im.append(c2[NB:])
        left = jnp.concatenate(prods, axis=0)
        right = jnp.concatenate(c_re + c_im, axis=0)
        gram = lax.dot_general(
            left, right, (((1,), (1,)), ((), ())), preferred_element_type=jnp.float32
        )
        diag = gram[: 2 * NB]
        for s in range(1, GROUP):
            diag = jnp.where(lane_group == s, gram[2 * NB * s : 2 * NB * (s + 1)], diag)
        real = diag[:NB, :LANES] + diag[NB:, LANES:]
        imag = diag[:NB, LANES:] - diag[NB:, :LANES]
        half_turn = LANES // 2
        even = jnp.where(low, real, pltpu.roll(imag, half_turn, 1))
        odd = jnp.where(low, pltpu.roll(real, half_turn, 1), imag)
        if c == 0:
            acc[2 * half, owner] = even
            acc[2 * half + 1, owner] = odd
        else:
            acc[2 * half, owner] += even
            acc[2 * half + 1, owner] += odd

    def across(off):
        peer = partner(col, off, ns)
        return pltpu.make_async_remote_copy(
            src_ref=acc.at[peer],
            dst_ref=part.at[off - 1],
            send_sem=send1.at[off - 1],
            recv_sem=recv1.at[off - 1],
            device_id=(me, peer),
            device_id_type=MESH,
        )

    for c in range(comps):
        if first:
            spectra(c, 0)
            spread(c, 0, stage)

            def arrive(i, carry, c=c):
                off = turn(i)
                exchange(c, off).wait_recv()
                spread(c, off, recv)
                return carry

            lax.fori_loop(0, n - 1, arrive, 0)
        else:
            own(c).wait()

            def arrive(off, carry, c=c):
                exchange(c, off).wait_recv()
                return carry

            lax.fori_loop(1, n, arrive, 0)

            def transform(b, carry, c=c):
                dft(c, b)
                return carry

            lax.fori_loop(0, NB, transform, 0)

        lax.fori_loop(0, bins, regroup, 0, unroll=4)

        for j in range(per_owner):
            half = lax.rem(col // 2 + 1 + j, per_owner)

            def grams(owner, carry, c=c, half=half):
                gram_group(c, owner, half)
                return carry

            lax.fori_loop(0, n, grams, 0, unroll=2)
            if c == comps - 1:
                for off in (2, 3) if j == 0 else (1,):
                    across(off).start()

    for off in range(1, ns):
        across(off).wait_recv()
    total = acc[col]
    for off in range(1, ns):
        total = total + part[off - 1]
    summed[...] = total

    def along(off):
        peer = partner(me, off, n)
        return pltpu.make_async_remote_copy(
            src_ref=summed.at[peer],
            dst_ref=last.at[off],
            send_sem=send2.at[off],
            recv_sem=recv2.at[off],
            device_id=(peer, col),
            device_id_type=MESH,
        )

    def begin2(off, carry):
        along(off).start()
        return carry

    lax.fori_loop(1, n, begin2, 0)

    def add2(off, total):
        along(off).wait_recv()
        return total + last[off]

    summed_all = lax.fori_loop(1, n, add2, summed[me])
    out[...] = summed_all * filled[col, pl.ds(me, 1), :]

    for off in range(1, ns):
        across(off).wait_send()

    def drain(off, carry):
        for c in range(comps):
            exchange(c, off).wait_send()
        along(off).wait_send()
        return carry

    lax.fori_loop(1, n, drain, 0)


def shards(n, ns, snapshots, cell_weights, triads, owner_slots):
    times, comps, cells = snapshots.shape
    owners, slot_count = owner_slots.shape
    weight_scale = 1.0 / math.sqrt(comps * cells * ns)
    vmem = pl.BlockSpec(memory_space=pltpu.VMEM)
    smem = pl.BlockSpec(memory_space=pltpu.SMEM)
    anywhere = pl.BlockSpec(memory_space=pl.ANY)
    sem = pltpu.SemaphoreType.DMA
    first = times % NT == 0
    blocks = times // NT

    def call(which, bins, *operands):
        if first:
            local = pltpu.VMEM((comps, times, n * LANES), jnp.bfloat16)
            stage = pltpu.VMEM((comps, n, blocks * 2 * bins, LANES), jnp.bfloat16)
            recv = stage
        else:
            local = stage = pltpu.VMEM((16, LANES), jnp.bfloat16)
            recv = pltpu.VMEM((comps, NB * NT, LANES), jnp.bfloat16)
        return pl.pallas_call(
            functools.partial(kernel, n, ns, weight_scale, bins),
            out_shape=jax.ShapeDtypeStruct((NB, LANES), jnp.float32),
            in_specs=[anywhere, anywhere, vmem, vmem, smem, vmem],
            out_specs=vmem,
            scratch_shapes=[
                pltpu.VMEM((2 * K, NT), jnp.bfloat16),
                pltpu.VMEM(((2 * bins + 15) // 16 * 16, NT), jnp.bfloat16),
                local,
                stage,
                recv,
                pltpu.VMEM((2 * bins * NB, LANES), jnp.float32),
                pltpu.VMEM((bins, 2 * NB, LANES), jnp.float32),
                pltpu.VMEM((bins, 2 * NB, LANES), jnp.bfloat16),
                pltpu.VMEM((ns, n, NB, LANES), jnp.float32),
                pltpu.VMEM((ns - 1, n, NB, LANES), jnp.float32),
                pltpu.VMEM((n, NB, LANES), jnp.float32),
                pltpu.VMEM((n, NB, LANES), jnp.float32),
                sem((comps, n)),
                sem((comps, n)),
                sem((comps,)),
                sem,
                sem((ns - 1,)),
                sem((ns - 1,)),
                sem((n,)),
                sem((n,)),
            ],
            compiler_params=pltpu.CompilerParams(
                collective_id=which,
                has_side_effects=True,
                vmem_limit_bytes=58 * 1024 * 1024,
            ),
        )(*operands)

    table = jnp.asarray(spectral_table())
    snap = snapshots.transpose(1, 0, 2)
    weights = cell_weights.reshape(n, LANES)
    mine = slot_count // ns
    if first:
        sizes = (92, 96, 100, 104, 108, K)
        place, freqs, filled, which = pl.pallas_call(
            functools.partial(choose, ns, sizes),
            out_shape=(
                jax.ShapeDtypeStruct((1, 2 * K), jnp.int32),
                jax.ShapeDtypeStruct((3, owners * slot_count), jnp.int32),
                jax.ShapeDtypeStruct((ns, owners, LANES), jnp.float32),
                jax.ShapeDtypeStruct((1, 1), jnp.int32),
            ),
            in_specs=[vmem, vmem],
            out_specs=(vmem, vmem, vmem, smem),
        )(triads.T, owner_slots)
        tile = lax.switch(
            which[0, 0],
            [functools.partial(call, i, bins) for i, bins in enumerate(sizes)],
            snap,
            table,
            place,
            weights,
            freqs,
            filled,
        )
    else:
        flat = owner_slots.reshape(-1)
        freqs = jnp.take(triads.T, jnp.maximum(flat, 0), axis=1, mode="clip")
        filled = (owner_slots >= 0).astype(jnp.float32).reshape(owners, ns, mine)
        filled = jnp.tile(jnp.repeat(filled.transpose(1, 0, 2), NB, axis=2), (1, 1, 2))
        place = jnp.zeros((1, 2 * K), jnp.int32)
        tile = call(0, K, snap, table, place, weights, freqs, filled)
    return (
        tile.reshape(NB, 2, mine, NB).transpose(2, 1, 0, 3).reshape(mine, 2 * NB * NB)
    )


def solution(mesh):
    placed = (P("tm", None, "space"), P("space"), P(), P())
    n, ns = mesh.shape["tm"], mesh.shape["space"]
    return jax.shard_map(
        functools.partial(shards, n, ns),
        mesh=mesh,
        in_specs=placed,
        out_specs=P(("tm", "space"), None),
        check_vma=False,
    )
```

profile of v0, /device:TPU:0, one launch (start us, length us, event | category | flops | bytes accessed | tf_op | source)
XLA Modules:
  0.0 74.9 jit_solution(3632081912006710445)
XLA Ops:
  0.0 1.5 %shard_map.55 = (s32[1,256]{1,0:T(1,128)S(1)}, s32[3,128]{1,0:T(4,128)S(1)}, f32[4,8,128]{2,1,0:T(8,128)S(1)}, s32[1,1]{1,0:T(1,128)}) custom-call(s32[3,64]{1,0:T(4,128)} %bitcast.22, s32[8,16]{1,0:T(8,128)} %slots.1), custom_call_target="tpu_custom_call" | custom-call | tf_op jit(solution)/shard_map/pallas_call | solution.py:438
  2.2 71.9 %conditional.1 = (f32[16,128]{1,0:T(8,128)S(1)}) conditional(s32[]{:T(128)} %bitcast.1, (bf16[3,512,1024]{2,1,0:T(8,128)(2,1)}, bf16[256,256]{1,0:T(8,128)(2,1)}, s32[1,256]{1,0:T(1,128)S(1)}, f32[8,128]{1,0:T(8,128)}, s32[3,128]{1,0:T(4,128)S(1)}, /*index=5*/f32[4,8,128]{2,1,0:T(8,128)S(1)}) %tuple.36, ...), branch_computations={%region_0.0_spmd, %region_1.0_spmd, %region_2.0_spmd, %region_3.0_... | conditional | bytes 8 | solution.py:449
  2.2 71.7 %branch_2_fun.1 = f32[16,128]{1,0:T(8,128)S(1)} custom-call(bf16[3,512,1024]{2,1,0:T(8,128)(2,1)} %get-tuple-element.96.snap, bf16[256,256]{1,0:T(8,128)(2,1)} %get-tuple-element.97.table, s32[1,256]{1,0:T(1,128)S(1)} %get-tuple-element.98.place, f32[8,128]{1,0:T(8,128)} %get-tuple-element.99.weights, s32[3,128]{1,0:T(4,128)S(1)} %get-tuple-element.100.freqs, ...), custom_call_target="tpu_custom_call" | custom-call | tf_op jit(solution)/shard_map/cond/branch_2_fun/pallas_call | solution.py:398
  74.1 0.1 reshape.13
  74.2 0.7 reshape.14
  (1 shorter events, 0.0 us)
where the time goes:
time: 76.1 us; the launch traced here: 74.9 us
  Pallas kernels  73.2 us (96%)
  local copies, waits for them, and re-layouts  0.81 us (1%)
    pallas_call x1, Pallas kernels, call(): pl.pallas_call(functools.partial(kernel, n, ns, weight_scale, bins), out_...  71.7 us

commit v1 on v0

--- a/solution.py
+++ b/solution.py
@@ -328,7 +328,7 @@
                 gram_group(c, owner, half)
                 return carry
 
-            lax.fori_loop(0, n, grams, 0, unroll=2)
+            lax.fori_loop(0, n, grams, 0, unroll=4)
             if c == comps - 1:
                 for off in (2, 3) if j == 0 else (1,):
                     across(off).start()

time: 76.1 us -> 75.7 us (level)
  no operation moved by 1% of the time
where the time goes in v1:
time: 75.7 us; the launch traced here: 74.4 us
  Pallas kernels  72.7 us (96%)
  local copies, waits for them, and re-layouts  0.81 us (1%)
    pallas_call x1, Pallas kernels, call(): pl.pallas_call(functools.partial(kernel, n, ns, weight_scale, bins), out_...  71.2 us

profile of v1, /device:TPU:0, one launch (start us, length us, event | category | flops | bytes accessed | tf_op | source)
XLA Modules:
  0.0 74.4 jit_solution(16620486667484859936)
XLA Ops:
  0.0 1.5 %shard_map.55 = (s32[1,256]{1,0:T(1,128)S(1)}, s32[3,128]{1,0:T(4,128)S(1)}, f32[4,8,128]{2,1,0:T(8,128)S(1)}, s32[1,1]{1,0:T(1,128)}) custom-call(s32[3,64]{1,0:T(4,128)} %bitcast.22, s32[8,16]{1,0:T(8,128)} %slots.1), custom_call_target="tpu_custom_call" | custom-call | tf_op jit(solution)/shard_map/pallas_call | solution.py:438
  2.2 71.4 %conditional.1 = (f32[16,128]{1,0:T(8,128)S(1)}) conditional(s32[]{:T(128)} %bitcast.1, (bf16[3,512,1024]{2,1,0:T(8,128)(2,1)}, bf16[256,256]{1,0:T(8,128)(2,1)}, s32[1,256]{1,0:T(1,128)S(1)}, f32[8,128]{1,0:T(8,128)}, s32[3,128]{1,0:T(4,128)S(1)}, /*index=5*/f32[4,8,128]{2,1,0:T(8,128)S(1)}) %tuple.36, ...), branch_computations={%region_0.0_spmd, %region_1.0_spmd, %region_2.0_spmd, %region_3.0_... | conditional | bytes 8 | solution.py:449
  2.2 71.2 %branch_2_fun.1 = f32[16,128]{1,0:T(8,128)S(1)} custom-call(bf16[3,512,1024]{2,1,0:T(8,128)(2,1)} %get-tuple-element.96.snap, bf16[256,256]{1,0:T(8,128)(2,1)} %get-tuple-element.97.table, s32[1,256]{1,0:T(1,128)S(1)} %get-tuple-element.98.place, f32[8,128]{1,0:T(8,128)} %get-tuple-element.99.weights, s32[3,128]{1,0:T(4,128)S(1)} %get-tuple-element.100.freqs, ...), custom_call_target="tpu_custom_call" | custom-call | tf_op jit(solution)/shard_map/cond/branch_2_fun/pallas_call | solution.py:398
  73.6 0.1 reshape.13
  73.7 0.7 reshape.14
  (1 shorter events, 0.0 us)
